TPU v7x, 32 devices: a whole 2x2x4 slice. The times are simulated.
32 devices in a mesh: blk: 4 (over y, x), grp: 8 (over z, core).
Axes of the slice: x: 2, y: 2, z: 4, core: 2. Of those that a mesh axis runs over, the one named last changes fastest.
Arguments:
- batch: bfloat16 [512, 768], P('blk'), may hold values from -6 to 6
- targets: float32 [512, 512], P('blk'), may hold values from -6 to 6
- centers: bfloat16 [32768, 768], P(('blk', 'grp')), may hold values from -6 to 6
- weights: float32 [32768, 512], P(('blk', 'grp')), may hold values from -96 to 96
- eigvec: float32 [2048, 160], P(('blk', 'grp')), may hold values from -0.625 to 0.625
- eig_scale: float32 [160], replicated, may hold values from 0.05 to 0.95
- step: float32 [1], replicated, may hold values from 488.28125 to 1464.8438
Outputs:
- predictions: float32 [512, 512], P('blk')
- new_weights: float32 [32768, 512], P(('blk', 'grp'))
All inputs are finite; a program needn't handle non-finite values.
Results may differ from a plain program's by a relative error of at most 0.00075.
Values may be sent and summed in bfloat16 or wider, within the bound.
A program may use at most 64 MiB of HBM per device.

v0:
```python
import functools

import jax
import jax.numpy as jnp
from jax import lax
from jax.experimental import pallas as pl
from jax.experimental.pallas import tpu as pltpu
from jax.sharding import PartitionSpec as P

MESH = pl.DeviceIdType.MESH
F32 = jnp.float32
BF16 = jnp.bfloat16
LANES = 128


def split(v):
    hi = v.astype(BF16)
    return hi, (v - hi.astype(F32)).astype(BF16)


def dot(a, b):
    return jnp.dot(a, b, preferred_element_type=F32)


def dot_nt(a, b):
    return lax.dot_general(a, b, (((1,), (1,)), ((), ())), preferred_element_type=F32)


def kernel(
    n, nz,
    batch, targets, centers, weights, eigvec, eig_t, eig_scale, step,
    pred_out, new_out,
    xall, w_hi, w_lo, csq, ktf, k_hi, k_lo, pall, mall, pc, mc, pb, mb, acc, macc, zb, mz,
    pred, rall, mfull,
    bxs, bxr, fxs, fxr, cps, cpr, cms, cmr, bps, bpr, bms, bmr, zps, zpr, zms, zmr,
    prs, prr, pxs, pxr, grs, grr, gbs, gbr, gms, gmr, frs, frr, fms, fmr,
):
    b0 = lax.axis_index("blk")
    g = lax.axis_index("grp")
    c = lax.rem(g, 2)
    zz = lax.div(g, 2)
    sib = g + 1 - 2 * c
    rows = batch.shape[0]
    half = rows // 2
    q = eig_t.shape[0]
    qh = q // 2
    nys = eigvec.shape[0]
    d = batch.shape[1]
    outs = weights.shape[1]
    ncol = min(nz, outs // LANES)
    cw = outs // ncol
    nrow = nz // ncol
    rz = half // nrow
    mine = pl.ds(pl.multiple_of(c * half, half), half)
    other = pl.ds(pl.multiple_of((1 - c) * half, half), half)
    qmine = pl.ds(pl.multiple_of(c * qh, qh), qh)
    qother = pl.ds(pl.multiple_of((1 - c) * qh, qh), qh)

    def copy(src, dst, ss, rs, to):
        return pltpu.make_async_remote_copy(
            src_ref=src, dst_ref=dst, send_sem=ss, recv_sem=rs, device_id=to, device_id_type=MESH
        )

    def fwd(k):
        return lax.rem(b0 + k, n)

    def back(k):
        return lax.rem(b0 + n - k, n)

    def zdev(z):
        return (b0, z * 2 + c)

    barrier = pltpu.get_barrier_semaphore()
    for k in range(1, n):
        pl.semaphore_signal(barrier, inc=1, device_id=(fwd(k), g), device_id_type=MESH)
    for k in range(1, nz):
        pl.semaphore_signal(barrier, inc=1, device_id=zdev(lax.rem(zz + k, nz)), device_id_type=MESH)
    pl.semaphore_signal(barrier, inc=1, device_id=(b0, sib), device_id_type=MESH)
    pl.semaphore_wait(barrier, n + nz - 1)

    def bx(k):
        return copy(batch.at[mine], xall.at[b0, mine], bxs.at[k], bxr.at[k], (fwd(k), g))

    for k in range(1, n):
        bx(k).start()

    wv = weights[...]
    hi, lo = split(wv)
    w_hi[...] = hi
    w_lo[...] = lo
    cen_sq = jnp.sum(centers[...].astype(F32) ** 2, axis=1, keepdims=True)
    csq[...] = jnp.broadcast_to(cen_sq, (cen_sq.shape[0], rows)).T

    def fx(k):
        p = back(k)
        return copy(xall.at[p, mine], xall.at[p, mine], fxs.at[k], fxr.at[k], (b0, sib))

    def cp(k):
        p = back(k)
        return copy(pall.at[p, other], pc.at[p], cps.at[k], cpr.at[k], (b0, sib))

    def cm(k):
        p = back(k)
        return copy(mall.at[p, qother], mc.at[p], cms.at[k], cmr.at[k], (b0, sib))

    def bp(k):
        p = back(k)
        return copy(pall.at[p, mine], pb.at[b0], bps.at[k], bpr.at[k], (p, g))

    def bm(k):
        p = back(k)
        return copy(mall.at[p, qmine], mb.at[b0], bms.at[k], bmr.at[k], (p, g))

    def chunk(k, x):
        p = back(k)
        x_sq = jnp.sum(x.astype(F32) ** 2, axis=1, keepdims=True)
        dist = csq[...] + x_sq - 2.0 * dot_nt(x, centers[...])
        kt = jnp.exp(-dist * (4.0 / d))
        ktf[p] = kt
        khi, klo = split(kt)
        both = dot(jnp.concatenate([khi, klo], axis=0), w_hi[...])
        pall[p] = both[:rows] + both[rows:] + dot(khi, w_lo[...])
        mall[p] = dot_nt(eig_t[...].astype(BF16), khi[:, :nys]).astype(BF16)
        cp(k).start()
        cm(k).start()

    def core_sum(k):
        p = back(k)
        cp(k).wait()
        cm(k).wait()
        pall[p, mine] = pall[p, mine] + pc[p]
        mall[p, qmine] = (mall[p, qmine].astype(F32) + mc[p].astype(F32)).astype(BF16)

    chunk(0, batch[...])

    def relay(k, carry):
        bx(k).wait()
        fx(k).start()
        return carry

    lax.fori_loop(1, n, relay, 0)

    def work(k, carry):
        fx(k).wait()
        chunk(k, xall[back(k)])

        @pl.when(k >= 2)
        def _():
            core_sum(k - 1)
            bp(k - 1).start()
            bm(k - 1).start()

        return carry

    lax.fori_loop(1, n, work, 0)
    core_sum(n - 1)
    bp(n - 1).start()
    bm(n - 1).start()
    core_sum(0)

    def turn(p, carry):
        th, tl = split(ktf[p].T)
        at = pl.ds(pl.multiple_of(p * rows, rows), rows)
        k_hi[:, at] = th
        k_lo[:, at] = tl
        return carry

    lax.fori_loop(0, n, turn, 0)

    acc[...] = pall[b0, mine]
    macc[...] = mall[b0, qmine].astype(F32)

    def gather_sum(k, carry):
        s = fwd(k)
        bp(k).wait()
        bm(k).wait()
        acc[...] += pb[s]
        macc[...] += mb[s].astype(F32)
        return carry

    lax.fori_loop(1, n, gather_sum, 0)

    def rows_of(z):
        return pl.multiple_of(lax.div(z, ncol) * rz, rz)

    def cols_of(z):
        return pl.ds(pl.multiple_of(lax.rem(z, ncol) * cw, cw), cw)

    def zp(k):
        z = lax.rem(zz + k, nz)
        return copy(
            acc.at[pl.ds(rows_of(z), rz), cols_of(z)], zb.at[zz], zps.at[k], zpr.at[k], zdev(z)
        )

    def zm(k):
        z = lax.rem(zz + k, nz)
        return copy(mz.at[zz], mz.at[zz], zms.at[k], zmr.at[k], zdev(z))

    for k in range(1, nz):
        zp(k).start()
    mz[zz] = macc[...].astype(BF16)
    for k in range(1, nz):
        zm(k).start()
    total = acc[pl.ds(rows_of(zz), rz), cols_of(zz)]
    for k in range(1, nz):
        zp(k).wait()
        total = total + zb[lax.rem(zz + nz - k, nz)]
    my_rows = pl.ds(pl.multiple_of(c * half + rows_of(zz), rz), rz)
    my_cols = cols_of(zz)
    pred[my_rows, my_cols] = total
    rall[b0, my_rows, my_cols] = (total - targets[my_rows, my_cols]).astype(BF16)

    def gr(k):
        at = rall.at[b0, my_rows, my_cols]
        return copy(at, at, grs.at[k], grr.at[k], zdev(lax.rem(zz + k, nz)))

    def pr(k):
        at = pred.at[my_rows, my_cols]
        return copy(at, at, prs.at[k], prr.at[k], zdev(lax.rem(zz + k, nz)))

    for k in range(1, nz):
        gr(k).start()
    for k in range(1, nz):
        pr(k).start()
    msum = mz[zz].astype(F32)
    for k in range(1, nz):
        zm(k).wait()
        msum = msum + mz[lax.rem(zz + nz - k, nz)].astype(F32)
    mfull[b0, qmine] = msum.astype(BF16)

    def gm(k):
        at = mfull.at[b0, qmine]
        return copy(at, at, gms.at[k], gmr.at[k], (fwd(k), g))

    def gb(k):
        at = rall.at[b0, mine]
        return copy(at, at, gbs.at[k], gbr.at[k], (fwd(k), g))

    def fr(k):
        at = rall.at[back(k), mine]
        return copy(at, at, frs.at[k], frr.at[k], (b0, sib))

    def fm(k):
        at = mfull.at[back(k), qmine]
        return copy(at, at, fms.at[k], fmr.at[k], (b0, sib))

    for k in range(1, nz):
        gr(k).wait()
    for k in range(1, n):
        gb(k).start()
    for k in range(1, n):
        gm(k).start()
    fr(0).start()
    fm(0).start()
    for k in range(1, n):
        gb(k).wait()
        fr(k).start()
        gm(k).wait()
        fm(k).start()
    for k in range(1, nz):
        pr(k).wait()
    px = copy(pred.at[mine], pred.at[mine], pxs, pxr, (b0, sib))
    px.start()
    for k in range(n):
        fr(k).wait()
        fm(k).wait()

    res = rall[...].reshape(n * rows, outs)
    rate = step[0]
    tile = 256 if weights.shape[0] % 256 == 0 else nys

    def update(t, carry):
        at = pl.ds(pl.multiple_of(t * tile, tile), tile)
        grad = dot(k_hi[at, :], res) + dot(k_lo[at, :], res)
        new_out[at, :] = weights[at, :] - rate * grad
        return carry

    lax.fori_loop(0, weights.shape[0] // tile, update, 0)
    proj = dot(mfull[0], rall[0])
    for p in range(1, n):
        proj = proj + dot(mfull[p], rall[p])
    corr = jnp.dot(
        eigvec[...], eig_scale[...] * proj, precision=lax.Precision.HIGHEST,
        preferred_element_type=F32,
    )
    new_out[:nys, :] = new_out[:nys, :] + rate * corr
    px.wait()
    pred_out[...] = pred[...]


def local(n, nz, batch, targets, centers, weights, eigvec, eig_scale, step):
    rows, d = batch.shape
    cen, outs = weights.shape
    q = eigvec.shape[1]
    half, qh = rows // 2, q // 2
    ncol = min(nz, outs // LANES)
    rz, cw = half // (nz // ncol), outs // ncol
    vmem = pl.BlockSpec(memory_space=pltpu.VMEM)
    dma = pltpu.SemaphoreType.DMA
    return pl.pallas_call(
        functools.partial(kernel, n, nz),
        out_shape=(
            jax.ShapeDtypeStruct((rows, outs), F32),
            jax.ShapeDtypeStruct((cen, outs), F32),
        ),
        in_specs=[vmem] * 7 + [pl.BlockSpec(memory_space=pltpu.SMEM)],
        out_specs=(vmem, vmem),
        scratch_shapes=[
            pltpu.VMEM((n, rows, d), BF16),
            pltpu.VMEM((cen, outs), BF16),
            pltpu.VMEM((cen, outs), BF16),
            pltpu.VMEM((rows, cen), F32),
            pltpu.VMEM((n, rows, cen), F32),
            pltpu.VMEM((cen, n * rows), BF16),
            pltpu.VMEM((cen, n * rows), BF16),
            pltpu.VMEM((n, rows, outs), F32),
            pltpu.VMEM((n, q, rows), BF16),
            pltpu.VMEM((n, half, outs), F32),
            pltpu.VMEM((n, qh, rows), BF16),
            pltpu.VMEM((n, half, outs), F32),
            pltpu.VMEM((n, qh, rows), BF16),
            pltpu.VMEM((half, outs), F32),
            pltpu.VMEM((qh, rows), F32),
            pltpu.VMEM((nz, rz, cw), F32),
            pltpu.VMEM((nz, qh, rows), BF16),
            pltpu.VMEM((rows, outs), F32),
            pltpu.VMEM((n, rows, outs), BF16),
            pltpu.VMEM((n, q, rows), BF16),
        ]
        + [dma((n,))] * 12
        + [dma((nz,))] * 6
        + [dma(()), dma(())]
        + [dma((nz,))] * 2
        + [dma((n,))] * 8,
        compiler_params=pltpu.CompilerParams(
            collective_id=0, has_side_effects=True, vmem_limit_bytes=48 * 1024 * 1024
        ),
        cost_estimate=pl.CostEstimate(
            flops=10 * cen * n * rows * outs, bytes_accessed=12 * cen * outs,
            transcendentals=cen * n * rows,
        ),
    )(batch, targets, centers, weights, eigvec, eigvec.T, eig_scale[:, None], step)


def solution(mesh):
    n, nz = mesh.shape["blk"], mesh.shape["grp"] // 2
    return jax.shard_map(
        functools.partial(local, n, nz),
        mesh=mesh,
        in_specs=(
            P("blk", None),
            P("blk", None),
            P(("blk", "grp"), None),
            P(("blk", "grp"), None),
            P(("blk", "grp"), None),
            P(),
            P(),
        ),
        out_specs=(P("blk", None), P(("blk", "grp"), None)),
        check_vma=False,
    )
```

profile of v0, /device:TPU:0, one launch (start us, length us, event | category | flops | bytes accessed | tf_op | source)
XLA Modules:
  0.0 52.9 jit_solution(7922948438494031227)
XLA Ops:
  1.3 0.8 %copy.11.eig_scale = f32[160,1]{1,0:T(8,128)S(1)} copy(f32[160,1]{0,1:T(1,128)} %bitcast.3) | data formatting | bytes 1280 | tf_op jit(solution)/shard_map/broadcast_in_dim | solution.py:342
  2.1 0.9 %copy.10 = f32[64,160]{0,1:T(8,128)S(1)} copy(f32[64,160]{1,0:T(8,128)} %eigvec.1) | data formatting | bytes 81920 | tf_op args[4]
  3.0 0.0 copy-start
  3.0 0.8 %copy-done = f32[64,160]{1,0:T(8,128)S(1)} copy-done((f32[64,160]{1,0:T(8,128)S(1)}, f32[64,160]{1,0:T(8,128)}, u32[]{:S(2)}) %copy-start) | copy-done | bytes 40984
  3.9 0.0 copy-start.1
  3.9 1.4 %copy-done.1 = bf16[1024,768]{1,0:T(8,128)(2,1)S(1)} copy-done((bf16[1024,768]{1,0:T(8,128)(2,1)S(1)}, bf16[1024,768]{1,0:T(8,128)(2,1)}, u32[]{:S(2)}) %copy-start.1) | copy-done | bytes 1572888
  5.3 0.0 copy-start.2
  5.3 0.9 %copy-done.2 = f32[128,512]{1,0:T(8,128)S(1)} copy-done((f32[128,512]{1,0:T(8,128)S(1)}, f32[128,512]{1,0:T(8,128)}, u32[]{:S(2)}) %copy-start.2) | copy-done | bytes 262168
  6.2 0.0 copy-start.3
  6.2 0.9 %copy-done.3 = bf16[128,768]{1,0:T(8,128)(2,1)S(1)} copy-done((bf16[128,768]{1,0:T(8,128)(2,1)S(1)}, bf16[128,768]{1,0:T(8,128)(2,1)}, u32[]{:S(2)}) %copy-start.3) | copy-done | bytes 196632
  7.1 43.7 %shard_map.86 = (f32[128,512]{1,0:T(8,128)S(1)}, f32[1024,512]{1,0:T(8,128)S(1)}) custom-call(bf16[128,768]{1,0:T(8,128)(2,1)S(1)} %copy-done.3, f32[128,512]{1,0:T(8,128)S(1)} %copy-done.2, bf16[1024,768]{1,0:T(8,128)(2,1)S(1)} %copy-done.1, f32[1024,512]{1,0:T(8,128)} %weights.1, f32[64,160]{1,0:T(8,128)S(1)} %copy-done, f32[160,64]{1,0:T(8,128)S(1)} %bitcast.2, ...), custom_call_target="tpu_custom_call" | custom-call | flops 2684354560 | bytes 6291456 | tf_op jit(solution)/shard_map/pallas_call | solution.py:300
  50.9 0.7 %copy.15 = f32[128,512]{1,0:T(8,128)} copy(f32[128,512]{1,0:T(8,128)S(1)} %get-tuple-element.4) | data formatting | bytes 524288
  51.6 1.3 %copy.16 = f32[1024,512]{1,0:T(8,128)} copy(f32[1024,512]{1,0:T(8,128)S(1)} %get-tuple-element.5) | data formatting | bytes 4194304
Async XLA Ops:
  3.0 0.8 %copy-start = (f32[64,160]{1,0:T(8,128)S(1)}, f32[64,160]{1,0:T(8,128)}, u32[]{:S(2)}) copy-start(f32[64,160]{1,0:T(8,128)} %eigvec.1) | copy-start | bytes 122884
  3.9 1.4 %copy-start.1 = (bf16[1024,768]{1,0:T(8,128)(2,1)S(1)}, bf16[1024,768]{1,0:T(8,128)(2,1)}, u32[]{:S(2)}) copy-start(bf16[1024,768]{1,0:T(8,128)(2,1)} %centers.1) | copy-start | bytes 4718596
  5.3 0.9 %copy-start.2 = (f32[128,512]{1,0:T(8,128)S(1)}, f32[128,512]{1,0:T(8,128)}, u32[]{:S(2)}) copy-start(f32[128,512]{1,0:T(8,128)} %targets.1) | copy-start | bytes 786436
  6.2 0.9 %copy-start.3 = (bf16[128,768]{1,0:T(8,128)(2,1)S(1)}, bf16[128,768]{1,0:T(8,128)(2,1)}, u32[]{:S(2)}) copy-start(bf16[128,768]{1,0:T(8,128)(2,1)} %batch.1) | copy-start | bytes 589828
where the time goes:
time: 53.3 us; the launch traced here: 52.9 us
  Pallas kernels  43.7 us (82%)
  local copies, waits for them, and re-layouts  7.86 us (15%)
  between operations  1.31 us (2%)
    pallas_call x1, Pallas kernels, local(): pl.pallas_call(functools.partial(kernel, n, nz), out_shape=(jax.ShapeDtyp...  43.7 us
    unnamed x11, local copies, waits for them, and re-layouts  7.08 us

commit v1 on v0

--- a/solution.py
+++ b/solution.py
@@ -28,12 +28,13 @@
 
 def kernel(
     n, nz,
-    batch, targets, centers, weights, eigvec, eig_t, eig_scale, step,
+    batch_h, targets_h, centers_h, weights_h, eigvec_h, scale_h, step,
     pred_out, new_out,
+    batch, targets, centers, weights, eigvec, eig_scale,
     xall, w_hi, w_lo, csq, ktf, k_hi, k_lo, pall, mall, pc, mc, pb, mb, acc, macc, zb, mz,
     pred, rall, mfull,
     bxs, bxr, fxs, fxr, cps, cpr, cms, cmr, bps, bpr, bms, bmr, zps, zpr, zms, zmr,
-    prs, prr, pxs, pxr, grs, grr, gbs, gbr, gms, gmr, frs, frr, fms, fmr,
+    prs, prr, pxs, pxr, grs, grr, gbs, gbr, gms, gmr, frs, frr, fms, fmr, ins, outs_sem,
 ):
     b0 = lax.axis_index("blk")
     g = lax.axis_index("grp")
@@ -42,7 +43,7 @@
     sib = g + 1 - 2 * c
     rows = batch.shape[0]
     half = rows // 2
-    q = eig_t.shape[0]
+    q = eigvec.shape[1]
     qh = q // 2
     nys = eigvec.shape[0]
     d = batch.shape[1]
@@ -62,20 +63,40 @@
         )
 
     def fwd(k):
-        return lax.rem(b0 + k, n)
-
-    def back(k):
-        return lax.rem(b0 + n - k, n)
+        peer, bit = 0, 1
+        while bit < n:
+            peer = peer + lax.rem(lax.div(b0, bit) + lax.div(jnp.int32(k), bit), 2) * bit
+            bit *= 2
+        return peer
+
+    back = fwd
 
     def zdev(z):
         return (b0, z * 2 + c)
 
+    loads = [
+        pltpu.make_async_copy(src, dst, ins.at[i])
+        for i, (src, dst) in enumerate(
+            (
+                (batch_h, batch),
+                (centers_h, centers),
+                (weights_h, weights),
+                (eigvec_h, eigvec),
+                (scale_h, eig_scale),
+                (targets_h, targets),
+            )
+        )
+    ]
+    for load in loads:
+        load.start()
+
     barrier = pltpu.get_barrier_semaphore()
     for k in range(1, n):
         pl.semaphore_signal(barrier, inc=1, device_id=(fwd(k), g), device_id_type=MESH)
     for k in range(1, nz):
         pl.semaphore_signal(barrier, inc=1, device_id=zdev(lax.rem(zz + k, nz)), device_id_type=MESH)
     pl.semaphore_signal(barrier, inc=1, device_id=(b0, sib), device_id_type=MESH)
+    loads[0].wait()
     pl.semaphore_wait(barrier, n + nz - 1)
 
     def bx(k):
@@ -84,6 +105,9 @@
     for k in range(1, n):
         bx(k).start()
 
+    for load in loads[1:]:
+        load.wait()
+    eig_t = eigvec[...].T.astype(BF16)
     wv = weights[...]
     hi, lo = split(wv)
     w_hi[...] = hi
@@ -120,7 +144,7 @@
         khi, klo = split(kt)
         both = dot(jnp.concatenate([khi, klo], axis=0), w_hi[...])
         pall[p] = both[:rows] + both[rows:] + dot(khi, w_lo[...])
-        mall[p] = dot_nt(eig_t[...].astype(BF16), khi[:, :nys]).astype(BF16)
+        mall[p] = dot_nt(eig_t, khi[:, :nys]).astype(BF16)
         cp(k).start()
         cm(k).start()
 
@@ -199,8 +223,6 @@
     for k in range(1, nz):
         zp(k).start()
     mz[zz] = macc[...].astype(BF16)
-    for k in range(1, nz):
-        zm(k).start()
     total = acc[pl.ds(rows_of(zz), rz), cols_of(zz)]
     for k in range(1, nz):
         zp(k).wait()
@@ -221,71 +243,94 @@
     for k in range(1, nz):
         gr(k).start()
     for k in range(1, nz):
-        pr(k).start()
+        zm(k).start()
+
+    def gm(k):
+        at = mfull.at[b0, qmine]
+        return copy(at, at, gms.at[k], gmr.at[k], (fwd(k), g))
+
+    def gb(k):
+        at = rall.at[b0, mine]
+        return copy(at, at, gbs.at[k], gbr.at[k], (fwd(k), g))
+
+    def fr(k):
+        at = rall.at[back(k), mine]
+        return copy(at, at, frs.at[k], frr.at[k], (b0, sib))
+
+    def fm(k):
+        at = mfull.at[back(k), qmine]
+        return copy(at, at, fms.at[k], fmr.at[k], (b0, sib))
+
+    for k in range(1, nz):
+        gr(k).wait()
+    for k in range(1, n):
+        gb(k).start()
+    fr(0).start()
     msum = mz[zz].astype(F32)
     for k in range(1, nz):
         zm(k).wait()
         msum = msum + mz[lax.rem(zz + nz - k, nz)].astype(F32)
     mfull[b0, qmine] = msum.astype(BF16)
-
-    def gm(k):
-        at = mfull.at[b0, qmine]
-        return copy(at, at, gms.at[k], gmr.at[k], (fwd(k), g))
-
-    def gb(k):
-        at = rall.at[b0, mine]
-        return copy(at, at, gbs.at[k], gbr.at[k], (fwd(k), g))
-
-    def fr(k):
-        at = rall.at[back(k), mine]
-        return copy(at, at, frs.at[k], frr.at[k], (b0, sib))
-
-    def fm(k):
-        at = mfull.at[back(k), qmine]
-        return copy(at, at, fms.at[k], fmr.at[k], (b0, sib))
-
-    for k in range(1, nz):
-        gr(k).wait()
-    for k in range(1, n):
-        gb(k).start()
-    for k in range(1, n):
-        gm(k).start()
-    fr(0).start()
-    fm(0).start()
+    for k in range(1, nz):
+        pr(k).start()
     for k in range(1, n):
         gb(k).wait()
         fr(k).start()
+    for k in range(1, n):
+        gm(k).start()
+    fm(0).start()
+    for k in range(n):
+        fr(k).wait()
+
+    res = rall[...].reshape(n * rows, outs)
+    rate = step[0]
+    tile = 256 if weights.shape[0] % 256 == 0 else nys
+    tiles = weights.shape[0] // tile
+
+    def put(t):
+        at = pl.ds(pl.multiple_of(t * tile, tile), tile)
+        return pltpu.make_async_copy(weights.at[at], new_out.at[at], outs_sem.at[t])
+
+    def update(t):
+        at = pl.ds(pl.multiple_of(t * tile, tile), tile)
+        grad = dot(k_hi[at, :], res) + dot(k_lo[at, :], res)
+        weights[at, :] = weights[at, :] - rate * grad
+
+    def update_out(t, carry):
+        update(t)
+        put(t).start()
+        return carry
+
+    lax.fori_loop(1, tiles, update_out, 0)
+    for k in range(1, n):
         gm(k).wait()
         fm(k).start()
     for k in range(1, nz):
         pr(k).wait()
     px = copy(pred.at[mine], pred.at[mine], pxs, pxr, (b0, sib))
     px.start()
+    update(jnp.int32(0))
     for k in range(n):
-        fr(k).wait()
         fm(k).wait()
-
-    res = rall[...].reshape(n * rows, outs)
-    rate = step[0]
-    tile = 256 if weights.shape[0] % 256 == 0 else nys
-
-    def update(t, carry):
-        at = pl.ds(pl.multiple_of(t * tile, tile), tile)
-        grad = dot(k_hi[at, :], res) + dot(k_lo[at, :], res)
-        new_out[at, :] = weights[at, :] - rate * grad
-        return carry
-
-    lax.fori_loop(0, weights.shape[0] // tile, update, 0)
     proj = dot(mfull[0], rall[0])
     for p in range(1, n):
         proj = proj + dot(mfull[p], rall[p])
     corr = jnp.dot(
-        eigvec[...], eig_scale[...] * proj, precision=lax.Precision.HIGHEST,
+        eigvec[...] * eig_scale[...], proj, precision=lax.Precision.HIGHEST,
         preferred_element_type=F32,
     )
-    new_out[:nys, :] = new_out[:nys, :] + rate * corr
+    weights[:nys, :] = weights[:nys, :] + rate * corr
+    put(jnp.int32(0)).start()
     px.wait()
-    pred_out[...] = pred[...]
+    put_pred = pltpu.make_async_copy(pred, pred_out, outs_sem.at[tiles])
+    put_pred.start()
+
+    def put_wait(t, carry):
+        put(t).wait()
+        return carry
+
+    lax.fori_loop(0, tiles, put_wait, 0)
+    put_pred.wait()
 
 
 def local(n, nz, batch, targets, centers, weights, eigvec, eig_scale, step):
@@ -295,7 +340,8 @@
     half, qh = rows // 2, q // 2
     ncol = min(nz, outs // LANES)
     rz, cw = half // (nz // ncol), outs // ncol
-    vmem = pl.BlockSpec(memory_space=pltpu.VMEM)
+    hbm = pl.BlockSpec(memory_space=pl.ANY)
+    tile = 256 if cen % 256 == 0 else eigvec.shape[0]
     dma = pltpu.SemaphoreType.DMA
     return pl.pallas_call(
         functools.partial(kernel, n, nz),
@@ -303,9 +349,15 @@
             jax.ShapeDtypeStruct((rows, outs), F32),
             jax.ShapeDtypeStruct((cen, outs), F32),
         ),
-        in_specs=[vmem] * 7 + [pl.BlockSpec(memory_space=pltpu.SMEM)],
-        out_specs=(vmem, vmem),
+        in_specs=[hbm] * 6 + [pl.BlockSpec(memory_space=pltpu.SMEM)],
+        out_specs=(hbm, hbm),
         scratch_shapes=[
+            pltpu.VMEM((rows, d), BF16),
+            pltpu.VMEM((rows, outs), F32),
+            pltpu.VMEM((cen, d), BF16),
+            pltpu.VMEM((cen, outs), F32),
+            pltpu.VMEM(eigvec.shape, F32),
+            pltpu.VMEM((1, q), F32),
             pltpu.VMEM((n, rows, d), BF16),
             pltpu.VMEM((cen, outs), BF16),
             pltpu.VMEM((cen, outs), BF16),
@@ -331,7 +383,8 @@
         + [dma((nz,))] * 6
         + [dma(()), dma(())]
         + [dma((nz,))] * 2
-        + [dma((n,))] * 8,
+        + [dma((n,))] * 8
+        + [dma((6,)), dma((cen // tile + 1,))],
         compiler_params=pltpu.CompilerParams(
             collective_id=0, has_side_effects=True, vmem_limit_bytes=48 * 1024 * 1024
         ),
@@ -339,7 +392,7 @@
             flops=10 * cen * n * rows * outs, bytes_accessed=12 * cen * outs,
             transcendentals=cen * n * rows,
         ),
-    )(batch, targets, centers, weights, eigvec, eigvec.T, eig_scale[:, None], step)
+    )(batch, targets, centers, weights, eigvec, eig_scale[None, :], step)
 
 
 def solution(mesh):

time: 53.3 us -> 51.8 us (0.972)
  local copies, waits for them, and re-layouts: 7.86 us -> 6.82 us
    broadcast_in_dim x1 -> x0, local copies, waits for them, and re-layouts: 0.78 us -> none  [local(): eig_scale[:, None]]
    unnamed x11 -> x12, local copies, waits for them, and re-layouts: 7.08 us -> 6.82 us
where the time goes in v1:
time: 51.8 us; the launch traced here: 51.5 us
  Pallas kernels  43.4 us (84%)
  local copies, waits for them, and re-layouts  6.82 us (13%)
  between operations  1.3 us (3%)
    pallas_call x1, Pallas kernels, local(): pl.pallas_call(functools.partial(kernel, n, nz), out_shape=(jax.ShapeDtyp...  43.4 us
    unnamed x12, local copies, waits for them, and re-layouts  6.82 us

profile of v1, /device:TPU:0, one launch (start us, length us, event | category | flops | bytes accessed | tf_op | source)
XLA Modules:
  0.0 51.5 jit_solution(15679054357742311534)
XLA Ops:
  1.3 0.0 copy-start
  1.3 1.4 %copy-done = bf16[1024,768]{1,0:T(8,128)(2,1)S(1)} copy-done((bf16[1024,768]{1,0:T(8,128)(2,1)S(1)}, bf16[1024,768]{1,0:T(8,128)(2,1)}, u32[]{:S(2)}) %copy-start) | copy-done | bytes 1572888
  2.7 0.0 copy-start.1
  2.7 0.9 %copy-done.1 = f32[128,512]{1,0:T(8,128)S(1)} copy-done((f32[128,512]{1,0:T(8,128)S(1)}, f32[128,512]{1,0:T(8,128)}, u32[]{:S(2)}) %copy-start.1) | copy-done | bytes 262168
  3.6 0.0 copy-start.2
  3.6 0.9 %copy-done.2 = bf16[128,768]{1,0:T(8,128)(2,1)S(1)} copy-done((bf16[128,768]{1,0:T(8,128)(2,1)S(1)}, bf16[128,768]{1,0:T(8,128)(2,1)}, u32[]{:S(2)}) %copy-start.2) | copy-done | bytes 196632
  4.6 0.0 copy-start.3
  4.6 0.8 %copy-done.3 = f32[64,160]{1,0:T(8,128)S(1)} copy-done((f32[64,160]{1,0:T(8,128)S(1)}, f32[64,160]{1,0:T(8,128)}, u32[]{:S(2)}) %copy-start.3) | copy-done | bytes 40984
  5.4 0.0 copy-start.4
  5.4 0.7 %copy-done.4 = f32[160]{0:T(256)S(1)} copy-done((f32[160]{0:T(256)S(1)}, f32[160]{0:T(256)}, u32[]{:S(2)}) %copy-start.4) | copy-done | bytes 664
  6.1 43.4 %shard_map.86 = (f32[128,512]{1,0:T(8,128)S(1)}, f32[1024,512]{1,0:T(8,128)S(1)}) custom-call(bf16[128,768]{1,0:T(8,128)(2,1)S(1)} %copy-done.2, f32[128,512]{1,0:T(8,128)S(1)} %copy-done.1, bf16[1024,768]{1,0:T(8,128)(2,1)S(1)} %copy-done, f32[1024,512]{1,0:T(8,128)} %weights_h.1, f32[64,160]{1,0:T(8,128)S(1)} %copy-done.3, f32[1,160]{1,0:T(1,128)S(1)} %bitcast.1, ...), custom_call_target="tpu_custom_call" | custom-call | flops 2684354560 | bytes 6291456 | tf_op jit(solution)/shard_map/pallas_call | solution.py:346
  49.5 0.7 %copy.12 = f32[128,512]{1,0:T(8,128)} copy(f32[128,512]{1,0:T(8,128)S(1)} %get-tuple-element.4) | data formatting | bytes 524288
  50.2 1.3 %copy.13 = f32[1024,512]{1,0:T(8,128)} copy(f32[1024,512]{1,0:T(8,128)S(1)} %get-tuple-element.5) | data formatting | bytes 4194304
Async XLA Ops:
  1.3 1.4 %copy-start = (bf16[1024,768]{1,0:T(8,128)(2,1)S(1)}, bf16[1024,768]{1,0:T(8,128)(2,1)}, u32[]{:S(2)}) copy-start(bf16[1024,768]{1,0:T(8,128)(2,1)} %centers_h.1) | copy-start | bytes 4718596
  2.7 0.9 %copy-start.1 = (f32[128,512]{1,0:T(8,128)S(1)}, f32[128,512]{1,0:T(8,128)}, u32[]{:S(2)}) copy-start(f32[128,512]{1,0:T(8,128)} %targets_h.1) | copy-start | bytes 786436
  3.6 0.9 %copy-start.2 = (bf16[128,768]{1,0:T(8,128)(2,1)S(1)}, bf16[128,768]{1,0:T(8,128)(2,1)}, u32[]{:S(2)}) copy-start(bf16[128,768]{1,0:T(8,128)(2,1)} %batch_h.1) | copy-start | bytes 589828
  4.6 0.8 %copy-start.3 = (f32[64,160]{1,0:T(8,128)S(1)}, f32[64,160]{1,0:T(8,128)}, u32[]{:S(2)}) copy-start(f32[64,160]{1,0:T(8,128)} %eigvec_h.1) | copy-start | bytes 122884
  5.4 0.7 %copy-start.4 = (f32[160]{0:T(256)S(1)}, f32[160]{0:T(256)}, u32[]{:S(2)}) copy-start(f32[160]{0:T(256)} %param.12) | copy-start | bytes 1924

commit v2 on v1

--- a/solution.py
+++ b/solution.py
@@ -157,16 +157,20 @@
 
     chunk(0, batch[...])
 
-    def relay(k, carry):
+    def relay(k):
         bx(k).wait()
         fx(k).start()
-        return carry
-
-    lax.fori_loop(1, n, relay, 0)
+
+    for k in range(1, min(3, n)):
+        relay(k)
 
     def work(k, carry):
         fx(k).wait()
         chunk(k, xall[back(k)])
+
+        @pl.when(k + 2 < n)
+        def _():
+            relay(k + 2)
 
         @pl.when(k >= 2)
         def _():
@@ -242,16 +246,22 @@
 
     for k in range(1, nz):
         gr(k).start()
-    for k in range(1, nz):
-        zm(k).start()
-
     def gm(k):
         at = mfull.at[b0, qmine]
         return copy(at, at, gms.at[k], gmr.at[k], (fwd(k), g))
 
-    def gb(k):
-        at = rall.at[b0, mine]
-        return copy(at, at, gbs.at[k], gbr.at[k], (fwd(k), g))
+    def gb(k, j):
+        z = lax.rem(zz + nz - j, nz)
+        at = rall.at[
+            b0, pl.ds(pl.multiple_of(c * half + rows_of(z), rz), rz), cols_of(z)
+        ]
+        return copy(at, at, gbs.at[j * n + k], gbr.at[j * n + k], (fwd(k), g))
+
+    def gb_send(j, carry):
+        gr(j).wait()
+        for k in range(1, n):
+            gb(k, j).start()
+        return carry
 
     def fr(k):
         at = rall.at[back(k), mine]
@@ -261,24 +271,30 @@
         at = mfull.at[back(k), qmine]
         return copy(at, at, fms.at[k], fmr.at[k], (b0, sib))
 
-    for k in range(1, nz):
-        gr(k).wait()
     for k in range(1, n):
-        gb(k).start()
+        gb(k, 0).start()
+    for k in range(1, nz):
+        zm(k).start()
+    lax.fori_loop(1, nz, gb_send, 0)
     fr(0).start()
     msum = mz[zz].astype(F32)
     for k in range(1, nz):
         zm(k).wait()
         msum = msum + mz[lax.rem(zz + nz - k, nz)].astype(F32)
     mfull[b0, qmine] = msum.astype(BF16)
-    for k in range(1, nz):
-        pr(k).start()
-    for k in range(1, n):
-        gb(k).wait()
-        fr(k).start()
     for k in range(1, n):
         gm(k).start()
     fm(0).start()
+    for k in range(1, nz):
+        pr(k).start()
+
+    def gb_take(k, carry):
+        for j in range(nz):
+            gb(k, j).wait()
+        fr(k).start()
+        return carry
+
+    lax.fori_loop(1, n, gb_take, 0)
     for k in range(n):
         fr(k).wait()
 
@@ -340,7 +356,7 @@
     half, qh = rows // 2, q // 2
     ncol = min(nz, outs // LANES)
     rz, cw = half // (nz // ncol), outs // ncol
-    hbm = pl.BlockSpec(memory_space=pl.ANY)
+    hbm = pl.BlockSpec(memory_space=pltpu.HBM)
     tile = 256 if cen % 256 == 0 else eigvec.shape[0]
     dma = pltpu.SemaphoreType.DMA
     return pl.pallas_call(
@@ -383,10 +399,11 @@
         + [dma((nz,))] * 6
         + [dma(()), dma(())]
         + [dma((nz,))] * 2
-        + [dma((n,))] * 8
+        + [dma((n * nz,))] * 2
+        + [dma((n,))] * 6
         + [dma((6,)), dma((cen // tile + 1,))],
         compiler_params=pltpu.CompilerParams(
-            collective_id=0, has_side_effects=True, vmem_limit_bytes=48 * 1024 * 1024
+            collective_id=0, has_side_effects=True, vmem_limit_bytes=60 * 1024 * 1024
         ),
         cost_estimate=pl.CostEstimate(
             flops=10 * cen * n * rows * outs, bytes_accessed=12 * cen * outs,

time: 51.8 us -> 48 us (0.927)
  local copies, waits for them, and re-layouts: 6.82 us -> 4.75 us
  Pallas kernels: 43.4 us -> 41.7 us
    unnamed x12 -> x2, local copies, waits for them, and re-layouts: 6.82 us -> 4.75 us
    pallas_call x1, Pallas kernels: 43.4 us -> 41.7 us  [local(): pl.pallas_call(functools.partial(kernel, n, nz), out_shape=(jax.ShapeDtyp...]
where the time goes in v2:
time: 48 us; the launch traced here: 47.8 us
  Pallas kernels  41.7 us (87%)
  local copies, waits for them, and re-layouts  4.75 us (10%)
  between operations  1.29 us (3%)
    pallas_call x1, Pallas kernels, local(): pl.pallas_call(functools.partial(kernel, n, nz), out_shape=(jax.ShapeDtyp...  41.7 us
    unnamed x2, local copies, waits for them, and re-layouts  4.75 us

profile of v2, /device:TPU:0, one launch (start us, length us, event | category | flops | bytes accessed | tf_op | source)
XLA Modules:
  0.0 47.8 jit_solution(14844695274876782948)
XLA Ops:
  1.3 41.7 %shard_map.86 = (f32[128,512]{1,0:T(8,128)}, f32[1024,512]{1,0:T(8,128)}) custom-call(bf16[128,768]{1,0:T(8,128)(2,1)} %batch_h.1, f32[128,512]{1,0:T(8,128)} %targets_h.1, bf16[1024,768]{1,0:T(8,128)(2,1)} %centers_h.1, f32[1024,512]{1,0:T(8,128)} %weights_h.1, f32[64,160]{1,0:T(8,128)} %eigvec_h.1, f32[1,160]{1,0:T(1,128)} %bitcast.1, f32[1]{0:T(128)S(6)} %copy.11.step), custom_call_target="tpu_custom_call" | custom-call | flops 2684354560 | bytes 6291456 | tf_op jit(solution)/shard_map/pallas_call | solution.py:362
  43.0 1.7 %copy.12 = f32[128,512]{1,0:T(8,128)} copy(f32[128,512]{1,0:T(8,128)} %get-tuple-element.4) | data formatting | bytes 524288
  44.7 3.1 %copy.13 = f32[1024,512]{1,0:T(8,128)} copy(f32[1024,512]{1,0:T(8,128)} %get-tuple-element.5) | data formatting | bytes 4194304

commit v3 on v2

--- a/solution.py
+++ b/solution.py
@@ -90,6 +90,12 @@
     for load in loads:
         load.start()
 
+    def rows_of(z):
+        return pl.multiple_of(lax.div(z, ncol) * rz, rz)
+
+    def cols_of(z):
+        return pl.ds(pl.multiple_of(lax.rem(z, ncol) * cw, cw), cw)
+
     barrier = pltpu.get_barrier_semaphore()
     for k in range(1, n):
         pl.semaphore_signal(barrier, inc=1, device_id=(fwd(k), g), device_id_type=MESH)
@@ -127,9 +133,19 @@
         p = back(k)
         return copy(mall.at[p, qother], mc.at[p], cms.at[k], cmr.at[k], (b0, sib))
 
-    def bp(k):
-        p = back(k)
-        return copy(pall.at[p, mine], pb.at[b0], bps.at[k], bpr.at[k], (p, g))
+    def bp(k, j):
+        p, z = back(k), lax.rem(zz + j, nz)
+        at = pl.ds(pl.multiple_of(c * half + rows_of(z), rz), rz)
+        return copy(
+            pall.at[p, at, cols_of(z)],
+            pb.at[b0, pl.ds(rows_of(z), rz), cols_of(z)],
+            bps.at[j * n + k], bpr.at[j * n + k], (p, g),
+        )
+
+    def bp_send(k):
+        for j in list(range(1, nz)) + [0]:
+            bp(k, j).start()
+        bm(k).start()
 
     def bm(k):
         p = back(k)
@@ -175,15 +191,13 @@
         @pl.when(k >= 2)
         def _():
             core_sum(k - 1)
-            bp(k - 1).start()
-            bm(k - 1).start()
+            bp_send(k - 1)
 
         return carry
 
     lax.fori_loop(1, n, work, 0)
     core_sum(n - 1)
-    bp(n - 1).start()
-    bm(n - 1).start()
+    bp_send(n - 1)
     core_sum(0)
 
     def turn(p, carry):
@@ -193,26 +207,7 @@
         k_lo[:, at] = tl
         return carry
 
-    lax.fori_loop(0, n, turn, 0)
-
-    acc[...] = pall[b0, mine]
-    macc[...] = mall[b0, qmine].astype(F32)
-
-    def gather_sum(k, carry):
-        s = fwd(k)
-        bp(k).wait()
-        bm(k).wait()
-        acc[...] += pb[s]
-        macc[...] += mb[s].astype(F32)
-        return carry
-
-    lax.fori_loop(1, n, gather_sum, 0)
-
-    def rows_of(z):
-        return pl.multiple_of(lax.div(z, ncol) * rz, rz)
-
-    def cols_of(z):
-        return pl.ds(pl.multiple_of(lax.rem(z, ncol) * cw, cw), cw)
+    lax.fori_loop(0, n // 2, turn, 0)
 
     def zp(k):
         z = lax.rem(zz + k, nz)
@@ -224,10 +219,29 @@
         z = lax.rem(zz + k, nz)
         return copy(mz.at[zz], mz.at[zz], zms.at[k], zmr.at[k], zdev(z))
 
-    for k in range(1, nz):
-        zp(k).start()
+    def piece_sum(j):
+        z = lax.rem(zz + j, nz)
+        at = pl.ds(pl.multiple_of(c * half + rows_of(z), rz), rz)
+        total = pall[b0, at, cols_of(z)]
+        for k in range(1, n):
+            bp(k, j).wait()
+            total = total + pb[fwd(k), pl.ds(rows_of(z), rz), cols_of(z)]
+        return total
+
+    def piece_send(j, carry):
+        z = lax.rem(zz + j, nz)
+        acc[pl.ds(rows_of(z), rz), cols_of(z)] = piece_sum(j)
+        zp(j).start()
+        return carry
+
+    lax.fori_loop(1, nz, piece_send, 0)
+    total = piece_sum(0)
+    macc[...] = mall[b0, qmine].astype(F32)
+    for k in range(1, n):
+        bm(k).wait()
+        macc[...] += mb[fwd(k)].astype(F32)
     mz[zz] = macc[...].astype(BF16)
-    total = acc[pl.ds(rows_of(zz), rz), cols_of(zz)]
+    lax.fori_loop(n // 2, n, turn, 0)
     for k in range(1, nz):
         zp(k).wait()
         total = total + zb[lax.rem(zz + nz - k, nz)]
@@ -366,7 +380,7 @@
             jax.ShapeDtypeStruct((cen, outs), F32),
         ),
         in_specs=[hbm] * 6 + [pl.BlockSpec(memory_space=pltpu.SMEM)],
-        out_specs=(hbm, hbm),
+        out_specs=(pl.BlockSpec(memory_space=pl.ANY),) * 2,
         scratch_shapes=[
             pltpu.VMEM((rows, d), BF16),
             pltpu.VMEM((rows, outs), F32),
@@ -395,7 +409,9 @@
             pltpu.VMEM((n, rows, outs), BF16),
             pltpu.VMEM((n, q, rows), BF16),
         ]
-        + [dma((n,))] * 12
+        + [dma((n,))] * 8
+        + [dma((n * nz,))] * 2
+        + [dma((n,))] * 2
         + [dma((nz,))] * 6
         + [dma(()), dma(())]
         + [dma((nz,))] * 2
@@ -403,13 +419,19 @@
         + [dma((n,))] * 6
         + [dma((6,)), dma((cen // tile + 1,))],
         compiler_params=pltpu.CompilerParams(
-            collective_id=0, has_side_effects=True, vmem_limit_bytes=60 * 1024 * 1024
+            collective_id=0, has_side_effects=True, vmem_limit_bytes=48 * 1024 * 1024
         ),
         cost_estimate=pl.CostEstimate(
             flops=10 * cen * n * rows * outs, bytes_accessed=12 * cen * outs,
             transcendentals=cen * n * rows,
         ),
-    )(batch, targets, centers, weights, eigvec, eig_scale[None, :], step)
+    )(
+        *(
+            pltpu.with_memory_space_constraint(v, pltpu.HBM)
+            for v in (batch, targets, centers, weights, eigvec, eig_scale[None, :])
+        ),
+        step,
+    )
 
 
 def solution(mesh):

time: 48 us -> 43 us (0.90)
  local copies, waits for them, and re-layouts: 4.75 us -> 2.02 us
  Pallas kernels: 41.7 us -> 39.5 us
    unnamed x2, local copies, waits for them, and re-layouts: 4.75 us -> 2.02 us
    pallas_call x1, Pallas kernels: 41.7 us -> 39.5 us  [local(): pl.pallas_call(functools.partial(kernel, n, nz), out_shape=(jax.ShapeDtyp...]
where the time goes in v3:
time: 43 us; the launch traced here: 42.8 us
  Pallas kernels  39.5 us (92%)
  local copies, waits for them, and re-layouts  2.02 us (5%)
  between operations  1.29 us (3%)
    pallas_call x1, Pallas kernels, local(): pl.pallas_call(functools.partial(kernel, n, nz), out_shape=(jax.ShapeDtyp...  39.5 us
    unnamed x2, local copies, waits for them, and re-layouts  2.02 us

profile of v3, /device:TPU:0, one launch (start us, length us, event | category | flops | bytes accessed | tf_op | source)
XLA Modules:
  0.0 42.8 jit_solution(2483525107803606217)
XLA Ops:
  1.3 39.5 %shard_map.86 = (f32[128,512]{1,0:T(8,128)S(1)}, f32[1024,512]{1,0:T(8,128)S(1)}) custom-call(bf16[128,768]{1,0:T(8,128)(2,1)} %batch_h.1, f32[128,512]{1,0:T(8,128)} %targets_h.1, bf16[1024,768]{1,0:T(8,128)(2,1)} %centers_h.1, f32[1024,512]{1,0:T(8,128)} %weights_h.1, f32[64,160]{1,0:T(8,128)} %eigvec_h.1, f32[1,160]{1,0:T(1,128)} %bitcast.1, f32[1]{0:T(128)S(6)} %copy.11.step), custom_call_target="tpu_custom_call" | custom-call | flops 2684354560 | bytes 6291456 | tf_op jit(solution)/shard_map/pallas_call | solution.py:376
  40.8 0.7 %copy.12 = f32[128,512]{1,0:T(8,128)} copy(f32[128,512]{1,0:T(8,128)S(1)} %get-tuple-element.4) | data formatting | bytes 524288
  41.5 1.3 %copy.13 = f32[1024,512]{1,0:T(8,128)} copy(f32[1024,512]{1,0:T(8,128)S(1)} %get-tuple-element.5) | data formatting | bytes 4194304

commit v4 on v3

--- a/solution.py
+++ b/solution.py
@@ -31,10 +31,10 @@
     batch_h, targets_h, centers_h, weights_h, eigvec_h, scale_h, step,
     pred_out, new_out,
     batch, targets, centers, weights, eigvec, eig_scale,
-    xall, w_hi, w_lo, csq, ktf, k_hi, k_lo, pall, mall, pc, mc, pb, mb, acc, macc, zb, mz,
+    xall, w_hi, w_lo, csq, ktf, k_both, pall, mall, pc, mc, pb, mb, acc, macc, zb, mz,
     pred, rall, mfull,
     bxs, bxr, fxs, fxr, cps, cpr, cms, cmr, bps, bpr, bms, bmr, zps, zpr, zms, zmr,
-    prs, prr, pxs, pxr, grs, grr, gbs, gbr, gms, gmr, frs, frr, fms, fmr, ins, outs_sem,
+    prs, prr, pxs, pxr, grs, grr, gbs, gbr, gms, gmr, frs, frr, fms, fmr, ins,
 ):
     b0 = lax.axis_index("blk")
     g = lax.axis_index("grp")
@@ -202,9 +202,8 @@
 
     def turn(p, carry):
         th, tl = split(ktf[p].T)
-        at = pl.ds(pl.multiple_of(p * rows, rows), rows)
-        k_hi[:, at] = th
-        k_lo[:, at] = tl
+        k_both[p, :, :rows] = th
+        k_both[p, :, rows:] = tl
         return carry
 
     lax.fori_loop(0, n // 2, turn, 0)
@@ -302,44 +301,48 @@
     for k in range(1, nz):
         pr(k).start()
 
-    def gb_take(k, carry):
+    rate = step[0]
+    tile = 256 if weights.shape[0] % 256 == 0 else nys
+    tiles = weights.shape[0] // tile
+
+    def gb_take(k):
         for j in range(nz):
             gb(k, j).wait()
         fr(k).start()
-        return carry
-
-    lax.fori_loop(1, n, gb_take, 0)
-    for k in range(n):
+
+    def update(k, base):
+        p = back(k)
+        res = jnp.concatenate([rall[p], rall[p]], axis=0)
+
+        def one(t, carry):
+            at = pl.ds(pl.multiple_of(t * tile, tile), tile)
+            new_out[at, :] = base[at, :] - rate * dot(k_both[p, at, :], res)
+            return carry
+
+        lax.fori_loop(0, tiles, one, 0)
+
+    fr(0).wait()
+    update(0, weights)
+    for k in range(1, min(3, n)):
+        gb_take(k)
+
+    def add_chunk(k, carry):
         fr(k).wait()
-
-    res = rall[...].reshape(n * rows, outs)
-    rate = step[0]
-    tile = 256 if weights.shape[0] % 256 == 0 else nys
-    tiles = weights.shape[0] // tile
-
-    def put(t):
-        at = pl.ds(pl.multiple_of(t * tile, tile), tile)
-        return pltpu.make_async_copy(weights.at[at], new_out.at[at], outs_sem.at[t])
-
-    def update(t):
-        at = pl.ds(pl.multiple_of(t * tile, tile), tile)
-        grad = dot(k_hi[at, :], res) + dot(k_lo[at, :], res)
-        weights[at, :] = weights[at, :] - rate * grad
-
-    def update_out(t, carry):
-        update(t)
-        put(t).start()
-        return carry
-
-    lax.fori_loop(1, tiles, update_out, 0)
-    for k in range(1, n):
+        update(k, new_out)
+
+        @pl.when(k + 2 < n)
+        def _():
+            gb_take(k + 2)
+
         gm(k).wait()
         fm(k).start()
+        return carry
+
+    lax.fori_loop(1, n, add_chunk, 0)
     for k in range(1, nz):
         pr(k).wait()
     px = copy(pred.at[mine], pred.at[mine], pxs, pxr, (b0, sib))
     px.start()
-    update(jnp.int32(0))
     for k in range(n):
         fm(k).wait()
     proj = dot(mfull[0], rall[0])
@@ -349,18 +352,9 @@
         eigvec[...] * eig_scale[...], proj, precision=lax.Precision.HIGHEST,
         preferred_element_type=F32,
     )
-    weights[:nys, :] = weights[:nys, :] + rate * corr
-    put(jnp.int32(0)).start()
+    new_out[:nys, :] = new_out[:nys, :] + rate * corr
     px.wait()
-    put_pred = pltpu.make_async_copy(pred, pred_out, outs_sem.at[tiles])
-    put_pred.start()
-
-    def put_wait(t, carry):
-        put(t).wait()
-        return carry
-
-    lax.fori_loop(0, tiles, put_wait, 0)
-    put_pred.wait()
+    pred_out[...] = pred[...]
 
 
 def local(n, nz, batch, targets, centers, weights, eigvec, eig_scale, step):
@@ -371,7 +365,6 @@
     ncol = min(nz, outs // LANES)
     rz, cw = half // (nz // ncol), outs // ncol
     hbm = pl.BlockSpec(memory_space=pltpu.HBM)
-    tile = 256 if cen % 256 == 0 else eigvec.shape[0]
     dma = pltpu.SemaphoreType.DMA
     return pl.pallas_call(
         functools.partial(kernel, n, nz),
@@ -380,7 +373,7 @@
             jax.ShapeDtypeStruct((cen, outs), F32),
         ),
         in_specs=[hbm] * 6 + [pl.BlockSpec(memory_space=pltpu.SMEM)],
-        out_specs=(pl.BlockSpec(memory_space=pl.ANY),) * 2,
+        out_specs=(pl.BlockSpec(memory_space=pltpu.VMEM),) * 2,
         scratch_shapes=[
             pltpu.VMEM((rows, d), BF16),
             pltpu.VMEM((rows, outs), F32),
@@ -393,8 +386,7 @@
             pltpu.VMEM((cen, outs), BF16),
             pltpu.VMEM((rows, cen), F32),
             pltpu.VMEM((n, rows, cen), F32),
-            pltpu.VMEM((cen, n * rows), BF16),
-            pltpu.VMEM((cen, n * rows), BF16),
+            pltpu.VMEM((n, cen, 2 * rows), BF16),
             pltpu.VMEM((n, rows, outs), F32),
             pltpu.VMEM((n, q, rows), BF16),
             pltpu.VMEM((n, half, outs), F32),
@@ -417,7 +409,7 @@
         + [dma((nz,))] * 2
         + [dma((n * nz,))] * 2
         + [dma((n,))] * 6
-        + [dma((6,)), dma((cen // tile + 1,))],
+        + [dma((6,))],
         compiler_params=pltpu.CompilerParams(
             collective_id=0, has_side_effects=True, vmem_limit_bytes=48 * 1024 * 1024
         ),

time: 43 us -> 43.6 us (1.014)
  Pallas kernels: 39.5 us -> 40.2 us
    pallas_call x1, Pallas kernels: 39.5 us -> 40.2 us  [local(): pl.pallas_call(functools.partial(kernel, n, nz), out_shape=(jax.ShapeDtyp...]
where the time goes in v4:
time: 43.6 us; the launch traced here: 43.5 us
  Pallas kernels  40.2 us (92%)
  local copies, waits for them, and re-layouts  2.02 us (5%)
  between operations  1.29 us (3%)
    pallas_call x1, Pallas kernels, local(): pl.pallas_call(functools.partial(kernel, n, nz), out_shape=(jax.ShapeDtyp...  40.2 us
    unnamed x2, local copies, waits for them, and re-layouts  2.02 us

profile of v4, /device:TPU:0, one launch (start us, length us, event | category | flops | bytes accessed | tf_op | source)
XLA Modules:
  0.0 43.5 jit_solution(12789327654892825116)
XLA Ops:
  1.3 40.2 %shard_map.86 = (f32[128,512]{1,0:T(8,128)S(1)}, f32[1024,512]{1,0:T(8,128)S(1)}) custom-call(bf16[128,768]{1,0:T(8,128)(2,1)} %batch_h.1, f32[128,512]{1,0:T(8,128)} %targets_h.1, bf16[1024,768]{1,0:T(8,128)(2,1)} %centers_h.1, f32[1024,512]{1,0:T(8,128)} %weights_h.1, f32[64,160]{1,0:T(8,128)} %eigvec_h.1, f32[1,160]{1,0:T(1,128)} %bitcast.1, f32[1]{0:T(128)S(6)} %copy.11.step), custom_call_target="tpu_custom_call" | custom-call | flops 2684354560 | bytes 6291456 | tf_op jit(solution)/shard_map/pallas_call | solution.py:369
  41.4 0.7 %copy.12 = f32[128,512]{1,0:T(8,128)} copy(f32[128,512]{1,0:T(8,128)S(1)} %get-tuple-element.4) | data formatting | bytes 524288
  42.2 1.3 %copy.13 = f32[1024,512]{1,0:T(8,128)} copy(f32[1024,512]{1,0:T(8,128)S(1)} %get-tuple-element.5) | data formatting | bytes 4194304

commit v5 on v3

--- a/solution.py
+++ b/solution.py
@@ -34,7 +34,7 @@
     xall, w_hi, w_lo, csq, ktf, k_hi, k_lo, pall, mall, pc, mc, pb, mb, acc, macc, zb, mz,
     pred, rall, mfull,
     bxs, bxr, fxs, fxr, cps, cpr, cms, cmr, bps, bpr, bms, bmr, zps, zpr, zms, zmr,
-    prs, prr, pxs, pxr, grs, grr, gbs, gbr, gms, gmr, frs, frr, fms, fmr, ins, outs_sem,
+    prs, prr, pxs, pxr, grs, grr, gbs, gbr, gms, gmr, frs, frr, fms, fmr, ins,
 ):
     b0 = lax.axis_index("blk")
     g = lax.axis_index("grp")
@@ -207,7 +207,7 @@
         k_lo[:, at] = tl
         return carry
 
-    lax.fori_loop(0, n // 2, turn, 0)
+    lax.fori_loop(0, n // 4, turn, 0)
 
     def zp(k):
         z = lax.rem(zz + k, nz)
@@ -241,7 +241,7 @@
         bm(k).wait()
         macc[...] += mb[fwd(k)].astype(F32)
     mz[zz] = macc[...].astype(BF16)
-    lax.fori_loop(n // 2, n, turn, 0)
+    lax.fori_loop(n // 4, n // 2, turn, 0)
     for k in range(1, nz):
         zp(k).wait()
         total = total + zb[lax.rem(zz + nz - k, nz)]
@@ -302,6 +302,8 @@
     for k in range(1, nz):
         pr(k).start()
 
+    lax.fori_loop(n // 2, n, turn, 0)
+
     def gb_take(k, carry):
         for j in range(nz):
             gb(k, j).wait()
@@ -309,37 +311,27 @@
         return carry
 
     lax.fori_loop(1, n, gb_take, 0)
+    for k in range(1, n):
+        gm(k).wait()
+        fm(k).start()
+    for k in range(1, nz):
+        pr(k).wait()
+    px = copy(pred.at[mine], pred.at[mine], pxs, pxr, (b0, sib))
+    px.start()
     for k in range(n):
         fr(k).wait()
 
     res = rall[...].reshape(n * rows, outs)
     rate = step[0]
     tile = 256 if weights.shape[0] % 256 == 0 else nys
-    tiles = weights.shape[0] // tile
-
-    def put(t):
-        at = pl.ds(pl.multiple_of(t * tile, tile), tile)
-        return pltpu.make_async_copy(weights.at[at], new_out.at[at], outs_sem.at[t])
-
-    def update(t):
+
+    def update(t, carry):
         at = pl.ds(pl.multiple_of(t * tile, tile), tile)
         grad = dot(k_hi[at, :], res) + dot(k_lo[at, :], res)
-        weights[at, :] = weights[at, :] - rate * grad
-
-    def update_out(t, carry):
-        update(t)
-        put(t).start()
-        return carry
-
-    lax.fori_loop(1, tiles, update_out, 0)
-    for k in range(1, n):
-        gm(k).wait()
-        fm(k).start()
-    for k in range(1, nz):
-        pr(k).wait()
-    px = copy(pred.at[mine], pred.at[mine], pxs, pxr, (b0, sib))
-    px.start()
-    update(jnp.int32(0))
+        new_out[at, :] = weights[at, :] - rate * grad
+        return carry
+
+    lax.fori_loop(0, weights.shape[0] // tile, update, 0)
     for k in range(n):
         fm(k).wait()
     proj = dot(mfull[0], rall[0])
@@ -349,18 +341,9 @@
         eigvec[...] * eig_scale[...], proj, precision=lax.Precision.HIGHEST,
         preferred_element_type=F32,
     )
-    weights[:nys, :] = weights[:nys, :] + rate * corr
-    put(jnp.int32(0)).start()
+    new_out[:nys, :] = new_out[:nys, :] + rate * corr
     px.wait()
-    put_pred = pltpu.make_async_copy(pred, pred_out, outs_sem.at[tiles])
-    put_pred.start()
-
-    def put_wait(t, carry):
-        put(t).wait()
-        return carry
-
-    lax.fori_loop(0, tiles, put_wait, 0)
-    put_pred.wait()
+    pred_out[...] = pred[...]
 
 
 def local(n, nz, batch, targets, centers, weights, eigvec, eig_scale, step):
@@ -371,7 +354,6 @@
     ncol = min(nz, outs // LANES)
     rz, cw = half // (nz // ncol), outs // ncol
     hbm = pl.BlockSpec(memory_space=pltpu.HBM)
-    tile = 256 if cen % 256 == 0 else eigvec.shape[0]
     dma = pltpu.SemaphoreType.DMA
     return pl.pallas_call(
         functools.partial(kernel, n, nz),
@@ -380,7 +362,7 @@
             jax.ShapeDtypeStruct((cen, outs), F32),
         ),
         in_specs=[hbm] * 6 + [pl.BlockSpec(memory_space=pltpu.SMEM)],
-        out_specs=(pl.BlockSpec(memory_space=pl.ANY),) * 2,
+        out_specs=(pl.BlockSpec(memory_space=pltpu.VMEM),) * 2,
         scratch_shapes=[
             pltpu.VMEM((rows, d), BF16),
             pltpu.VMEM((rows, outs), F32),
@@ -417,7 +399,7 @@
         + [dma((nz,))] * 2
         + [dma((n * nz,))] * 2
         + [dma((n,))] * 6
-        + [dma((6,)), dma((cen // tile + 1,))],
+        + [dma((6,))],
         compiler_params=pltpu.CompilerParams(
             collective_id=0, has_side_effects=True, vmem_limit_bytes=48 * 1024 * 1024
         ),

time: 43 us -> 42.8 us (level)
  no operation moved by 1% of the time
where the time goes in v5:
time: 42.8 us; the launch traced here: 42.7 us
  Pallas kernels  39.4 us (92%)
  local copies, waits for them, and re-layouts  2.02 us (5%)
  between operations  1.29 us (3%)
    pallas_call x1, Pallas kernels, local(): pl.pallas_call(functools.partial(kernel, n, nz), out_shape=(jax.ShapeDtyp...  39.4 us
    unnamed x2, local copies, waits for them, and re-layouts  2.02 us

profile of v5, /device:TPU:0, one launch (start us, length us, event | category | flops | bytes accessed | tf_op | source)
XLA Modules:
  0.0 42.7 jit_solution(8072598114353598168)
XLA Ops:
  1.3 39.4 %shard_map.86 = (f32[128,512]{1,0:T(8,128)S(1)}, f32[1024,512]{1,0:T(8,128)S(1)}) custom-call(bf16[128,768]{1,0:T(8,128)(2,1)} %batch_h.1, f32[128,512]{1,0:T(8,128)} %targets_h.1, bf16[1024,768]{1,0:T(8,128)(2,1)} %centers_h.1, f32[1024,512]{1,0:T(8,128)} %weights_h.1, f32[64,160]{1,0:T(8,128)} %eigvec_h.1, f32[1,160]{1,0:T(1,128)} %bitcast.1, f32[1]{0:T(128)S(6)} %copy.11.step), custom_call_target="tpu_custom_call" | custom-call | flops 2684354560 | bytes 6291456 | tf_op jit(solution)/shard_map/pallas_call | solution.py:358
  40.7 0.7 %copy.12 = f32[128,512]{1,0:T(8,128)} copy(f32[128,512]{1,0:T(8,128)S(1)} %get-tuple-element.4) | data formatting | bytes 524288
  41.4 1.3 %copy.13 = f32[1024,512]{1,0:T(8,128)} copy(f32[1024,512]{1,0:T(8,128)S(1)} %get-tuple-element.5) | data formatting | bytes 4194304

commit v6 on v5

--- a/solution.py
+++ b/solution.py
@@ -108,7 +108,7 @@
     def bx(k):
         return copy(batch.at[mine], xall.at[b0, mine], bxs.at[k], bxr.at[k], (fwd(k), g))
 
-    for k in range(1, n):
+    for k in range(n - 1, 0, -1):
         bx(k).start()
 
     for load in loads[1:]:

time: 42.8 us -> 44.2 us (1.033)
  Pallas kernels: 39.4 us -> 40.7 us
    pallas_call x1, Pallas kernels: 39.4 us -> 40.7 us  [local(): pl.pallas_call(functools.partial(kernel, n, nz), out_shape=(jax.ShapeDtyp...]
where the time goes in v6:
time: 44.2 us; the launch traced here: 44 us
  Pallas kernels  40.7 us (92%)
  local copies, waits for them, and re-layouts  2.02 us (5%)
  between operations  1.29 us (3%)
    pallas_call x1, Pallas kernels, local(): pl.pallas_call(functools.partial(kernel, n, nz), out_shape=(jax.ShapeDtyp...  40.7 us
    unnamed x2, local copies, waits for them, and re-layouts  2.02 us

profile of v6, /device:TPU:0, one launch (start us, length us, event | category | flops | bytes accessed | tf_op | source)
XLA Modules:
  0.0 44.0 jit_solution(14958765084177531172)
XLA Ops:
  1.3 40.7 %shard_map.86 = (f32[128,512]{1,0:T(8,128)S(1)}, f32[1024,512]{1,0:T(8,128)S(1)}) custom-call(bf16[128,768]{1,0:T(8,128)(2,1)} %batch_h.1, f32[128,512]{1,0:T(8,128)} %targets_h.1, bf16[1024,768]{1,0:T(8,128)(2,1)} %centers_h.1, f32[1024,512]{1,0:T(8,128)} %weights_h.1, f32[64,160]{1,0:T(8,128)} %eigvec_h.1, f32[1,160]{1,0:T(1,128)} %bitcast.1, f32[1]{0:T(128)S(6)} %copy.11.step), custom_call_target="tpu_custom_call" | custom-call | flops 2684354560 | bytes 6291456 | tf_op jit(solution)/shard_map/pallas_call | solution.py:358
  42.0 0.7 %copy.12 = f32[128,512]{1,0:T(8,128)} copy(f32[128,512]{1,0:T(8,128)S(1)} %get-tuple-element.4) | data formatting | bytes 524288
  42.7 1.3 %copy.13 = f32[1024,512]{1,0:T(8,128)} copy(f32[1024,512]{1,0:T(8,128)S(1)} %get-tuple-element.5) | data formatting | bytes 4194304
